TPU v7x, 256 devices: a whole 4x4x8 slice. The times are simulated.
256 devices in a mesh: dp: 16 (over z, core), tensor: 16 (over y, x).
Axes of the slice: x: 4, y: 4, z: 8, core: 2. Of those that a mesh axis runs over, the one named last changes fastest.
Arguments:
- activations: bfloat16 [36864, 8192], P('dp', 'tensor'), may hold values from -6 to 6
- out_grads: bfloat16 [36864, 28672], P('dp', 'tensor'), may hold values from -0.0546875 to 0.0546875
- basis: bfloat16 [8192, 256], P('tensor'), may hold values from -0.375 to 0.375
- first_moment: float32 [256, 28672], P('dp', 'tensor'), may hold values from -6 to 6
- second_moment: float32 [256, 28672], P('dp', 'tensor'), may hold values from 0.05 to 0.8
- reward_codes: int32 [36864], P('dp'), may hold values from 0 to 15
- token_ids: int32 [36864], P('dp'), may hold values from 0 to 128004, as said below
Outputs:
- new_first: float32 [256, 28672], P('dp', 'tensor')
- new_second: float32 [256, 28672], P('dp', 'tensor')
- weight_update: bfloat16 [8192, 28672], P('dp', 'tensor')
Inputs may be any that keep to these rules, and one draw needn't show every extreme that they name: `token_ids`: the id 128004 is the padding token; the first of each 2304 consecutive tokens is never padding.
All inputs are finite; a program needn't handle non-finite values.
Results may differ from a plain program's by a relative error of at most 0.019.
Values may be sent and summed in bfloat16 or wider, within the bound.
A program may use at most 64 MiB of HBM per device.

v0:
```python
import jax
import jax.numpy as jnp
from jax import lax
from jax.sharding import PartitionSpec as P

ADAM_STEP = 100
pad_token = 128004
reward_temp = 0.2
beta_one = 0.9
beta_two = 0.999
adam_eps = 1e-08


def filled_up(lines, size):
    spare = -len(lines) % size
    return jnp.pad(lines, [(0, spare)] + [(0, 0)] * (lines.ndim - 1))


def joined_along(parts, dim):
    parts = jnp.moveaxis(parts, 0, dim)
    lengths = parts.shape
    return parts.reshape(*lengths[:dim], lengths[dim] * lengths[dim + 1], *lengths[dim + 2 :])


def sent_to_all(shard, axis):
    size = lax.axis_size(axis)
    return lax.all_to_all(
        jnp.broadcast_to(shard[None], (size, *shard.shape)), axis, 0, 0, tiled=True
    )


def gather_directly(shard, axis, dim):
    return joined_along(sent_to_all(shard, axis), dim)


def split_up(shard, dim, size):
    before, after = (shard.shape[:dim], shard.shape[dim + 1 :])
    return jnp.moveaxis(shard.reshape(*before, size, -1, *after), dim, 0)


def sum_at_owner(shard, axis, dim):
    parts = split_up(shard, dim, lax.axis_size(axis))
    arrived = lax.all_to_all(parts, axis, split_axis=0, concat_axis=0, tiled=True)
    return arrived.astype(jnp.float32).sum(axis=0)


def total_of(shard, axes):
    lines = shard.reshape(-1, shard.shape[-1])
    padded = filled_up(lines, lax.axis_size(axes))
    whole = gather_directly(sum_at_owner(padded, axes, 0).astype(jnp.bfloat16), axes, 0)
    return lax.slice_in_dim(whole, 0, len(lines)).reshape(shard.shape).astype(jnp.float32)


def of_everyone(shard, axis):
    return sent_to_all(shard, axis).sum(axis=0)


def broadcast(shard, axis, root):
    return lax.dynamic_index_in_dim(lax.all_gather(shard, axis), root, 0, keepdims=False)


def local(activations, out_grads, basis, first_moment, second_moment, reward_codes, token_ids):
    data_count = lax.axis_size("dp")
    tensor_count = lax.axis_size("tensor")
    partial_value = jnp.dot(activations, basis, preferred_element_type=jnp.float32)
    projected = total_of(partial_value.astype(jnp.bfloat16), "tensor")
    unmasked = (token_ids != pad_token).astype(jnp.float32)
    weights = unmasked * jnp.exp(reward_temp * reward_codes.astype(jnp.float32))
    local_total = jnp.sum(weights)
    weighted = (weights[:, None] * projected).astype(jnp.bfloat16)
    raw_grad = lax.dot_general(
        weighted, out_grads, (((0,), (0,)), ((), ())), preferred_element_type=jnp.float32
    )
    normalizer = of_everyone(local_total, "dp")
    grad_rows = sum_at_owner(raw_grad.astype(jnp.bfloat16), "dp", 0)
    token_count = activations.shape[0] * data_count
    gradient = grad_rows * (token_count / normalizer)
    new_first = beta_one * first_moment + (1.0 - beta_one) * gradient
    new_second = beta_two * second_moment + (1.0 - beta_two) * gradient * gradient
    bias_one = 1.0 - beta_one**ADAM_STEP
    bias_two = 1.0 - beta_two**ADAM_STEP
    update = (new_first / bias_one / (jnp.sqrt(new_second / bias_two) + adam_eps)).astype(
        jnp.bfloat16
    )
    data_index = lax.axis_index("dp")
    owner_index = data_index * tensor_count // data_count
    owner_rows = broadcast(basis, "tensor", owner_index)
    summed = jnp.dot(
        owner_rows,
        lax.all_gather(update, "dp", axis=0, tiled=True),
        preferred_element_type=jnp.float32,
    )
    return (new_first, new_second, summed.astype(jnp.bfloat16))


def solution(mesh):
    return jax.shard_map(
        local,
        mesh=mesh,
        in_specs=(
            P("dp", "tensor"),
            P("dp", "tensor"),
            P("tensor", None),
            P("dp", "tensor"),
            P("dp", "tensor"),
            P("dp"),
            P("dp"),
        ),
        out_specs=(P("dp", "tensor"), P("dp", "tensor"), P("dp", "tensor")),
        check_vma=False,
    )
```

profile of v0, /device:TPU:1, one launch (start us, length us, event | category | flops | bytes accessed | tf_op | source)
XLA Modules:
  0.0 148.8 jit_solution(3367582259047807124)
XLA Ops:
  7.2 0.0 copy-start
  7.2 0.0 all-gather.3.cloned.1.call-start
  7.2 0.7 all-gather.3.cloned.1.call-update
  7.9 0.9 copy-done
  8.8 1.7 %convolution_convert_fusion = bf16[2304,256]{1,0:T(8,128)(2,1)S(1)} fusion(bf16[2304,512]{1,0:T(8,128)(2,1)S(1)} %copy-done, bf16[512,256]{1,0:T(8,128)(2,1)} %param.9), kind=kOutput, calls=%fused_computation | convolution fusion | flops 604569600 | bytes 3801088 | tf_op jit(solution)/shard_map/dot_general | solution.py:65
  10.6 26.5 %all_to_all.21 = bf16[16,144,256]{2,1,0:T(8,128)(2,1)S(1)} all-to-all(bf16[16,144,256]{2,1,0:T(8,128)(2,1)S(1)} %bitcast.14), channel_id=1, replica_groups=mesh['dp'=16,'tensor'=16] {'tensor'}, dimensions={0} | all-to-all | bytes 2359296 | tf_op jit(solution)/shard_map/all_to_all | solution.py:43
  37.1 0.8 reduce_sum.39
  37.9 2.0 %broadcast_in_dim.4 = bf16[16,144,256]{2,1,0:T(8,128)(2,1)} broadcast(bf16[144,256]{1,0:T(8,128)(2,1)} %reduce_sum.39), dimensions={1,2} | broadcast | bytes 1253376 | tf_op jit(solution)/shard_map/broadcast_in_dim | solution.py:28
  39.9 3.7 %all-to-all-start.1 = ((bf16[16,144,256]{2,1,0:T(8,128)(2,1)}), bf16[16,144,256]{2,1,0:T(8,128)(2,1)S(1)}, u32[]{:S(2)}, u32[]{:S(2)}) async-start(bf16[16,144,256]{2,1,0:T(8,128)(2,1)} %broadcast_in_dim.4), calls=%async_computation.1 | async-start | bytes 2359296 | tf_op jit(solution)/shard_map/all_to_all | solution.py:27
  43.6 1.3 fusion.8
  44.9 14.6 %all-to-all-done.1 = bf16[16,144,256]{2,1,0:T(8,128)(2,1)S(1)} async-done(((bf16[16,144,256]{2,1,0:T(8,128)(2,1)}), bf16[16,144,256]{2,1,0:T(8,128)(2,1)S(1)}, u32[]{:S(2)}, u32[]{:S(2)}) %all-to-all-start.1) | async-done | bytes 1179680 | tf_op jit(solution)/shard_map/all_to_all | solution.py:27
  59.6 1.2 broadcast_in_dim.5
  60.8 21.0 %all-to-all-start.3 = ((f32[16,1,1]{2,1,0:T(1,128)}), f32[16,1,1]{2,1,0:T(1,128)}, u32[]{:S(2)}, u32[]{:S(2)}) async-start(f32[16,1,1]{2,1,0:T(1,128)} %broadcast_in_dim.5), calls=%async_computation.3 | async-start | bytes 16384 | tf_op jit(solution)/shard_map/all_to_all | solution.py:27
  81.9 6.7 %convolution_convert_fusion.2 = bf16[256,1792]{1,0:T(8,128)(2,1)} fusion(bf16[2304,1792]{1,0:T(8,128)(2,1)} %param.8, bf16[2304,256]{1,0:T(8,128)(2,1)S(1)} %bitcast.12, f32[2304]{0:T(1024)S(1)} %get-tuple-element.7), kind=kOutput, calls=%fused_computation.2 | convolution fusion | flops 2116157440 | bytes 10363904 | tf_op jit(solution)/shard_map/dot_general | solution.py:71
  88.6 0.3 all-to-all-done.3
  88.9 7.0 %all-to-all-start.2 = ((bf16[16,16,1792]{2,1,0:T(8,128)(2,1)}), bf16[16,16,1792]{2,1,0:T(8,128)(2,1)S(1)}, u32[]{:S(2)}, u32[]{:S(2)}) async-start(bf16[16,16,1792]{2,1,0:T(8,128)(2,1)} %bitcast.13), calls=%async_computation.2 | async-start | bytes 1835008 | tf_op jit(solution)/shard_map/all_to_all | solution.py:43
  96.0 1.3 reduce_sum.42
  98.0 23.3 %all-to-all-done.2 = bf16[16,16,1792]{2,1,0:T(8,128)(2,1)S(1)} async-done(((bf16[16,16,1792]{2,1,0:T(8,128)(2,1)}), bf16[16,16,1792]{2,1,0:T(8,128)(2,1)S(1)}, u32[]{:S(2)}, u32[]{:S(2)}) %all-to-all-start.2) | async-done | bytes 917536 | tf_op jit(solution)/shard_map/all_to_all | solution.py:43
  121.2 0.1 convert_reduce_fusion
  121.4 0.0 copy-done.1
  121.4 0.0 copy-done.2
  121.4 0.8 divide_convert_fusion
  122.2 17.0 %all_gather.11 = bf16[256,1792]{1,0:T(8,128)(2,1)S(1)} all-gather(bf16[16,1792]{1,0:T(8,128)(2,1)S(1)} %get-tuple-element.3), channel_id=1, replica_groups=mesh['dp'=16,'tensor'=16] {'dp'}, dimensions={0}, use_global_device_ids=true | all-gather | bytes 974848 | tf_op jit(solution)/shard_map/all_gather | solution.py:90
  139.1 2.8 %convolution_convert_fusion.1 = bf16[512,1792]{1,0:T(8,128)(2,1)} fusion(bf16[256,1792]{1,0:T(8,128)(2,1)S(1)} %all_gather.11, bf16[16,512,256]{2,1,0:T(8,128)(2,1)} %bitcast.15, s32[]{:T(128)S(6)} %select_n.10), kind=kOutput, calls=%fused_computation.1 | convolution fusion | flops 470679552 | bytes 3014660 | tf_op jit(solution)/shard_map/dot_general | solution.py:88
  (3 shorter events, 0.0 us)
Async XLA Ops:
  7.2 1.7 %copy-start = (bf16[2304,512]{1,0:T(8,128)(2,1)S(1)}, bf16[2304,512]{1,0:T(8,128)(2,1)}, u32[]{:S(2)}) copy-start(bf16[2304,512]{1,0:T(8,128)(2,1)} %param.7) | copy-start | bytes 7077892
  7.2 132.0 %all-gather.3.cloned.1.call-start = ((), (), s32[]{:S(2)}) async-start(), calls=%async_computation.4 | async-start | bytes 4456448 | tf_op jit(solution)/shard_map/all_gather | solution.py:59
  39.9 19.7 %all-to-all-start.1 = ((bf16[16,144,256]{2,1,0:T(8,128)(2,1)}), bf16[16,144,256]{2,1,0:T(8,128)(2,1)S(1)}, u32[]{:S(2)}, u32[]{:S(2)}) async-start(bf16[16,144,256]{2,1,0:T(8,128)(2,1)} %broadcast_in_dim.4), calls=%async_computation.1 | async-start | bytes 2359296 | tf_op jit(solution)/shard_map/all_to_all | solution.py:27
  60.8 28.1 %all-to-all-start.3 = ((f32[16,1,1]{2,1,0:T(1,128)}), f32[16,1,1]{2,1,0:T(1,128)}, u32[]{:S(2)}, u32[]{:S(2)}) async-start(f32[16,1,1]{2,1,0:T(1,128)} %broadcast_in_dim.5), calls=%async_computation.3 | async-start | bytes 16384 | tf_op jit(solution)/shard_map/all_to_all | solution.py:27
  88.6 32.8 %copy-start.1 = (f32[16,1792]{1,0:T(8,128)S(1)}, f32[16,1792]{1,0:T(8,128)}, u32[]{:S(2)}) copy-start(f32[16,1792]{1,0:T(8,128)} %param.11) | copy-start | bytes 344068
  88.6 32.8 %copy-start.2 = (f32[16,1792]{1,0:T(8,128)S(1)}, f32[16,1792]{1,0:T(8,128)}, u32[]{:S(2)}) copy-start(f32[16,1792]{1,0:T(8,128)} %param.10) | copy-start | bytes 344068
  88.9 32.3 %all-to-all-start.2 = ((bf16[16,16,1792]{2,1,0:T(8,128)(2,1)}), bf16[16,16,1792]{2,1,0:T(8,128)(2,1)S(1)}, u32[]{:S(2)}, u32[]{:S(2)}) async-start(bf16[16,16,1792]{2,1,0:T(8,128)(2,1)} %bitcast.13), calls=%async_computation.2 | async-start | bytes 1835008 | tf_op jit(solution)/shard_map/all_to_all | solution.py:43
Sparse Core Ops, SparseCore 0:
  10.4 67.8 all-gather.2
where the time goes:
time: 149 us
  blocking collectives  43.5 us (29%)
  waiting for transfers between devices  38.9 us (26%)
  starting transfers between devices  31.8 us (21%)
  between operations  14.8 us (10%)
  matrix products  11.3 us (8%)
  other arithmetic  4.34 us (3%)
  local copies, waits for them, and re-layouts  4.16 us (3%)
    all_to_all x1, blocking collectives, sum_at_owner(): lax.all_to_all(parts, axis, split_axis=0, concat_axis=0, tiled=True)  26.5 us
    all_to_all x2, starting transfers between devices, sent_to_all(): lax.all_to_all(jnp.broadcast_to(shard[None], (size, *shard.shape)), axis,...  24.7 us
    all_to_all x1, waiting for transfers between devices, sum_at_owner(): lax.all_to_all(parts, axis, split_axis=0, concat_axis=0, tiled=True)  23.3 us
    all_gather x1, blocking collectives, local(): lax.all_gather(update, 'dp', axis=0, tiled=True)  17 us
    all_to_all x2, waiting for transfers between devices, sent_to_all(): lax.all_to_all(jnp.broadcast_to(shard[None], (size, *shard.shape)), axis,...  15 us
    all_to_all x1, starting transfers between devices, sum_at_owner(): lax.all_to_all(parts, axis, split_axis=0, concat_axis=0, tiled=True)  7.04 us
    dot_general x1, matrix products, local(): lax.dot_general(weighted, out_grads, (((0,), (0,)), ((), ())), preferred_...  6.72 us
    broadcast_in_dim x2, local copies, waits for them, and re-layouts, sent_to_all(): jnp.broadcast_to(shard[None], (size, *shard.shape))  3.22 us
  transfers between devices with their start and end apart: 4, of which 3 were waited for; matrix products, arithmetic and copies ran while one was open for 11% of the time, Pallas kernels for 0%

commit v1 on v0

--- a/solution.py
+++ b/solution.py
@@ -9,6 +9,19 @@
 beta_one = 0.9
 beta_two = 0.999
 adam_eps = 1e-08
+
+
+def gather_around(x, axis, dim):
+    ways = lax.axis_size(axis)
+    up = [(d, (d + 1) % ways) for d in range(ways)]
+    down = [(d, (d - 1) % ways) for d in range(ways)]
+    earlier, later = ([x], [x])
+    for _ in range(ways // 2):
+        earlier.append(lax.ppermute(earlier[-1], axis, up))
+    for _ in range((ways - 1) // 2):
+        later.append(lax.ppermute(later[-1], axis, down))
+    line = jnp.concatenate([*earlier[::-1], *later[1:]], axis=dim)
+    return jnp.roll(line, (lax.axis_index(axis) - ways // 2) * x.shape[dim], axis=dim)
 
 
 def filled_up(lines, size):
@@ -85,11 +98,7 @@
     data_index = lax.axis_index("dp")
     owner_index = data_index * tensor_count // data_count
     owner_rows = broadcast(basis, "tensor", owner_index)
-    summed = jnp.dot(
-        owner_rows,
-        lax.all_gather(update, "dp", axis=0, tiled=True),
-        preferred_element_type=jnp.float32,
-    )
+    summed = jnp.dot(owner_rows, gather_around(update, "dp", 0), preferred_element_type=jnp.float32)
     return (new_first, new_second, summed.astype(jnp.bfloat16))
 
 

time: 149 us -> 177 us (1.19); the launches traced: 149 us -> 175 us
  local copies, waits for them, and re-layouts: 4.16 us -> 24.9 us
  blocking collectives: 43.5 us -> 24.8 us
  starting transfers between devices: 31.8 us -> 47.8 us
  waiting for transfers between devices: 38.9 us -> 46.8 us
    ppermute x0 -> x15, starting transfers between devices: none -> 24.9 us  [the longest x7 17.4 us: gather_around(): later.append(lax.ppermute(later[-1], axis, down))]
    unnamed x6 -> x37, local copies, waits for them, and re-layouts: 0.94 us -> 21 us
    all_gather x1 -> x0, blocking collectives: 17 us -> none  [local(): lax.all_gather(update, 'dp', axis=0, tiled=True)]
    all_to_all x2, starting transfers between devices: 24.7 us -> 15.7 us  [sent_to_all(): lax.all_to_all(jnp.broadcast_to(shard[None], (size, *shard.shape)), axis,...]
    ppermute x0 -> x15, waiting for transfers between devices: none -> 8.43 us  [the longest x8 5.06 us: gather_around(): earlier.append(lax.ppermute(earlier[-1], axis, up))]
  transfers between devices with their start and end apart: 4 -> 19, of which waited for: 3 -> 15; matrix products, arithmetic and copies ran while one was open for 11% -> 17% of each run, Pallas kernels for 0% -> 0%
where the time goes in v1:
time: 177 us; the launch traced here: 175 us
  starting transfers between devices  47.8 us (27%)
  waiting for transfers between devices  46.8 us (26%)
  local copies, waits for them, and re-layouts  24.9 us (14%)
  blocking collectives  24.8 us (14%)
  between operations  14.8 us (8%)
  matrix products  11.6 us (7%)
  other arithmetic  4.35 us (2%)
    all_to_all x1, blocking collectives, sum_at_owner(): lax.all_to_all(parts, axis, split_axis=0, concat_axis=0, tiled=True)  24.8 us
    all_to_all x1, waiting for transfers between devices, sum_at_owner(): lax.all_to_all(parts, axis, split_axis=0, concat_axis=0, tiled=True)  22.6 us
    unnamed x37, local copies, waits for them, and re-layouts  21 us
    ppermute x7, starting transfers between devices, gather_around(): later.append(lax.ppermute(later[-1], axis, down))  17.4 us
    all_to_all x2, starting transfers between devices, sent_to_all(): lax.all_to_all(jnp.broadcast_to(shard[None], (size, *shard.shape)), axis,...  15.7 us
    all_to_all x2, waiting for transfers between devices, sent_to_all(): lax.all_to_all(jnp.broadcast_to(shard[None], (size, *shard.shape)), axis,...  15.2 us
    ppermute x8, starting transfers between devices, gather_around(): earlier.append(lax.ppermute(earlier[-1], axis, up))  7.51 us
    all_to_all x1, starting transfers between devices, sum_at_owner(): lax.all_to_all(parts, axis, split_axis=0, concat_axis=0, tiled=True)  7.19 us
  transfers between devices with their start and end apart: 19, of which 15 were waited for; matrix products, arithmetic and copies ran while one was open for 17% of the time, Pallas kernels for 0%

profile of v1, /device:TPU:1, one launch (start us, length us, event | category | flops | bytes accessed | tf_op | source)
XLA Modules:
  0.0 175.0 jit_solution(14265469233357354165)
XLA Ops:
  7.2 1.7 copy-done
  8.8 1.7 convolution_convert_fusion
  10.6 24.8 %all_to_all.21 = bf16[16,144,256]{2,1,0:T(8,128)(2,1)S(1)} all-to-all(bf16[16,144,256]{2,1,0:T(8,128)(2,1)S(1)} %bitcast.13), channel_id=1, replica_groups=mesh['dp'=16,'tensor'=16] {'tensor'}, dimensions={0} | all-to-all | bytes 2359296 | tf_op jit(solution)/shard_map/all_to_all | solution.py:56
  36.2 2.0 %broadcast_in_dim.4 = bf16[16,144,256]{2,1,0:T(8,128)(2,1)} broadcast(bf16[144,256]{1,0:T(8,128)(2,1)} %reduce_sum.39), dimensions={1,2} | broadcast | bytes 1253376 | tf_op jit(solution)/shard_map/broadcast_in_dim | solution.py:41
  38.1 3.7 %all-to-all-start.1 = ((bf16[16,144,256]{2,1,0:T(8,128)(2,1)}), bf16[16,144,256]{2,1,0:T(8,128)(2,1)S(1)}, u32[]{:S(2)}, u32[]{:S(2)}) async-start(bf16[16,144,256]{2,1,0:T(8,128)(2,1)} %broadcast_in_dim.4), calls=%async_computation.1 | async-start | bytes 2359296 | tf_op jit(solution)/shard_map/all_to_all | solution.py:40
  41.9 1.3 fusion.9
  43.2 15.0 %all-to-all-done.1 = bf16[16,144,256]{2,1,0:T(8,128)(2,1)S(1)} async-done(((bf16[16,144,256]{2,1,0:T(8,128)(2,1)}), bf16[16,144,256]{2,1,0:T(8,128)(2,1)S(1)}, u32[]{:S(2)}, u32[]{:S(2)}) %all-to-all-start.1) | async-done | bytes 1179680 | tf_op jit(solution)/shard_map/all_to_all | solution.py:40
  58.2 1.2 broadcast_in_dim.5
  59.4 12.0 %all-to-all-start.3 = ((f32[16,1,1]{2,1,0:T(1,128)}), f32[16,1,1]{2,1,0:T(1,128)}, u32[]{:S(2)}, u32[]{:S(2)}) async-start(f32[16,1,1]{2,1,0:T(1,128)} %broadcast_in_dim.5), calls=%async_computation.3 | async-start | bytes 16384 | tf_op jit(solution)/shard_map/all_to_all | solution.py:40
  71.4 6.7 %convolution_convert_fusion.2 = bf16[256,1792]{1,0:T(8,128)(2,1)} fusion(bf16[2304,1792]{1,0:T(8,128)(2,1)} %param.8, bf16[2304,256]{1,0:T(8,128)(2,1)S(1)} %bitcast.11, f32[2304]{0:T(1024)S(1)} %get-tuple-element.7), kind=kOutput, calls=%fused_computation.2 | convolution fusion | flops 2116157440 | bytes 10363904 | tf_op jit(solution)/shard_map/dot_general | solution.py:84
  78.3 7.2 %all-to-all-start.2 = ((bf16[16,16,1792]{2,1,0:T(8,128)(2,1)}), bf16[16,16,1792]{2,1,0:T(8,128)(2,1)S(1)}, u32[]{:S(2)}, u32[]{:S(2)}) async-start(bf16[16,16,1792]{2,1,0:T(8,128)(2,1)} %bitcast.12), calls=%async_computation.2 | async-start | bytes 1835008 | tf_op jit(solution)/shard_map/all_to_all | solution.py:56
  86.2 1.3 reduce_sum.42
  88.2 22.6 %all-to-all-done.2 = bf16[16,16,1792]{2,1,0:T(8,128)(2,1)S(1)} async-done(((bf16[16,16,1792]{2,1,0:T(8,128)(2,1)}), bf16[16,16,1792]{2,1,0:T(8,128)(2,1)S(1)}, u32[]{:S(2)}, u32[]{:S(2)}) %all-to-all-start.2) | async-done | bytes 917536 | tf_op jit(solution)/shard_map/all_to_all | solution.py:56
  111.7 1.3 collective-permute-done
  113.0 2.3 %collective-permute-start.1 = (bf16[16,1792]{1,0:T(8,128)(2,1)S(1)}, bf16[16,1792]{1,0:T(8,128)(2,1)S(1)}, u32[]{:S(2)}, u32[]{:S(2)}) collective-permute-start(bf16[16,1792]{1,0:T(8,128)(2,1)S(1)} %collective-permute-done), channel_id=1, source_target_pairs={{0,16},{16,32},{32,48},{48,64},{64,80},{80,96},{96,112},{112,128},... | collective-permute-start | bytes 172040 | tf_op jit(solution)/shard_map/ppermute | solution.py:20
  115.3 1.3 collective-permute-done.1
  116.6 2.3 %collective-permute-start.2 = (bf16[16,1792]{1,0:T(8,128)(2,1)S(1)}, bf16[16,1792]{1,0:T(8,128)(2,1)S(1)}, u32[]{:S(2)}, u32[]{:S(2)}) collective-permute-start(bf16[16,1792]{1,0:T(8,128)(2,1)S(1)} %collective-permute-done.1), channel_id=1, source_target_pairs={{0,16},{16,32},{32,48},{48,64},{64,80},{80,96},{96,112},{112,128},... | collective-permute-start | bytes 172040 | tf_op jit(solution)/shard_map/ppermute | solution.py:20
  120.5 2.0 %collective-permute-start.3 = (bf16[16,1792]{1,0:T(8,128)(2,1)S(1)}, bf16[16,1792]{1,0:T(8,128)(2,1)S(1)}, u32[]{:S(2)}, u32[]{:S(2)}) collective-permute-start(bf16[16,1792]{1,0:T(8,128)(2,1)S(1)} %collective-permute-done.2), channel_id=1, source_target_pairs={{0,16},{16,32},{32,48},{48,64},{64,80},{80,96},{96,112},{112,128},... | collective-permute-start | bytes 172040 | tf_op jit(solution)/shard_map/ppermute | solution.py:20
  122.8 1.8 %collective-permute-start.10 = (bf16[16,1792]{1,0:T(8,128)(2,1)S(1)}, bf16[16,1792]{1,0:T(8,128)(2,1)S(1)}, u32[]{:S(2)}, u32[]{:S(2)}) collective-permute-start(bf16[16,1792]{1,0:T(8,128)(2,1)S(1)} %collective-permute-done.9), channel_id=1, source_target_pairs={{0,240},{16,0},{32,16},{48,32},{64,48},{80,64},{96,80},{112,96},{1... | collective-permute-start | bytes 172040 | tf_op jit(solution)/shard_map/ppermute | solution.py:22
  126.8 2.6 %collective-permute-start.11 = (bf16[16,1792]{1,0:T(8,128)(2,1)S(1)}, bf16[16,1792]{1,0:T(8,128)(2,1)S(1)}, u32[]{:S(2)}, u32[]{:S(2)}) collective-permute-start(bf16[16,1792]{1,0:T(8,128)(2,1)S(1)} %collective-permute-done.10), channel_id=1, source_target_pairs={{0,240},{16,0},{32,16},{48,32},{64,48},{80,64},{96,80},{112,96},{1... | collective-permute-start | bytes 172040 | tf_op jit(solution)/shard_map/ppermute | solution.py:22
  130.8 3.8 %collective-permute-start.12 = (bf16[16,1792]{1,0:T(8,128)(2,1)S(1)}, bf16[16,1792]{1,0:T(8,128)(2,1)S(1)}, u32[]{:S(2)}, u32[]{:S(2)}) collective-permute-start(bf16[16,1792]{1,0:T(8,128)(2,1)S(1)} %collective-permute-done.11), channel_id=1, source_target_pairs={{0,240},{16,0},{32,16},{48,32},{64,48},{80,64},{96,80},{112,96},{1... | collective-permute-start | bytes 172040 | tf_op jit(solution)/shard_map/ppermute | solution.py:22
  135.5 4.3 %collective-permute-start.13 = (bf16[16,1792]{1,0:T(8,128)(2,1)S(1)}, bf16[16,1792]{1,0:T(8,128)(2,1)S(1)}, u32[]{:S(2)}, u32[]{:S(2)}) collective-permute-start(bf16[16,1792]{1,0:T(8,128)(2,1)S(1)} %collective-permute-done.12), channel_id=1, source_target_pairs={{0,240},{16,0},{32,16},{48,32},{64,48},{80,64},{96,80},{112,96},{1... | collective-permute-start | bytes 172040 | tf_op jit(solution)/shard_map/ppermute | solution.py:22
  140.7 4.3 %collective-permute-start.14 = (bf16[16,1792]{1,0:T(8,128)(2,1)S(1)}, bf16[16,1792]{1,0:T(8,128)(2,1)S(1)}, u32[]{:S(2)}, u32[]{:S(2)}) collective-permute-start(bf16[16,1792]{1,0:T(8,128)(2,1)S(1)} %collective-permute-done.13), channel_id=1, source_target_pairs={{0,240},{16,0},{32,16},{48,32},{64,48},{80,64},{96,80},{112,96},{1... | collective-permute-start | bytes 172040 | tf_op jit(solution)/shard_map/ppermute | solution.py:22
  165.0 3.1 %convolution_convert_fusion.1 = bf16[512,1792]{1,0:T(8,128)(2,1)} fusion(bf16[512,1792]{1,0:T(8,128)(2,1)} %constant_dynamic-update-slice_fusion, s32[]{:T(128)S(6)} %select_n.24, bf16[16,512,256]{2,1,0:T(8,128)(2,1)} %bitcast.14, s32[]{:T(128)S(6)} %select_n.22), kind=kOutput, calls=%fused_computation.1 | convolution fusion | flops 470679552 | bytes 3014664 | tf_op jit(solution)/shard_map/dot_general | solution.py:101
  (64 shorter events, 29.9 us)
Async XLA Ops:
  7.2 1.7 copy-start
  38.1 20.1 %all-to-all-start.1 = ((bf16[16,144,256]{2,1,0:T(8,128)(2,1)}), bf16[16,144,256]{2,1,0:T(8,128)(2,1)S(1)}, u32[]{:S(2)}, u32[]{:S(2)}) async-start(bf16[16,144,256]{2,1,0:T(8,128)(2,1)} %broadcast_in_dim.4), calls=%async_computation.1 | async-start | bytes 2359296 | tf_op jit(solution)/shard_map/all_to_all | solution.py:40
  59.4 18.9 %all-to-all-start.3 = ((f32[16,1,1]{2,1,0:T(1,128)}), f32[16,1,1]{2,1,0:T(1,128)}, u32[]{:S(2)}, u32[]{:S(2)}) async-start(f32[16,1,1]{2,1,0:T(1,128)} %broadcast_in_dim.5), calls=%async_computation.3 | async-start | bytes 16384 | tf_op jit(solution)/shard_map/all_to_all | solution.py:40
  78.1 32.8 %copy-start.1 = (f32[16,1792]{1,0:T(8,128)S(1)}, f32[16,1792]{1,0:T(8,128)}, u32[]{:S(2)}) copy-start(f32[16,1792]{1,0:T(8,128)} %param.11) | copy-start | bytes 344068
  78.1 32.8 %copy-start.2 = (f32[16,1792]{1,0:T(8,128)S(1)}, f32[16,1792]{1,0:T(8,128)}, u32[]{:S(2)}) copy-start(f32[16,1792]{1,0:T(8,128)} %param.10) | copy-start | bytes 344068
  78.3 32.5 %all-to-all-start.2 = ((bf16[16,16,1792]{2,1,0:T(8,128)(2,1)}), bf16[16,16,1792]{2,1,0:T(8,128)(2,1)S(1)}, u32[]{:S(2)}, u32[]{:S(2)}) async-start(bf16[16,16,1792]{2,1,0:T(8,128)(2,1)} %bitcast.12), calls=%async_computation.2 | async-start | bytes 1835008 | tf_op jit(solution)/shard_map/all_to_all | solution.py:56
  85.5 79.5 %all-gather.3.cloned.1.call-start = ((), (), s32[]{:S(2)}) async-start(), calls=%async_computation.4 | async-start | bytes 4456448 | tf_op jit(solution)/shard_map/all_gather | solution.py:72
  111.7 1.3 collective-permute-start
  113.0 3.6 %collective-permute-start.1 = (bf16[16,1792]{1,0:T(8,128)(2,1)S(1)}, bf16[16,1792]{1,0:T(8,128)(2,1)S(1)}, u32[]{:S(2)}, u32[]{:S(2)}) collective-permute-start(bf16[16,1792]{1,0:T(8,128)(2,1)S(1)} %collective-permute-done), channel_id=1, source_target_pairs={{0,16},{16,32},{32,48},{48,64},{64,80},{80,96},{96,112},{112,128},... | collective-permute-start | bytes 172040 | tf_op jit(solution)/shard_map/ppermute | solution.py:20
  115.3 3.9 %collective-permute-start.8 = (bf16[16,1792]{1,0:T(8,128)(2,1)S(1)}, bf16[16,1792]{1,0:T(8,128)(2,1)S(1)}, u32[]{:S(2)}, u32[]{:S(2)}) collective-permute-start(bf16[16,1792]{1,0:T(8,128)(2,1)S(1)} %get-tuple-element.3), channel_id=1, source_target_pairs={{0,240},{16,0},{32,16},{48,32},{64,48},{80,64},{96,80},{112,96},{1... | collective-permute-start | bytes 172040 | tf_op jit(solution)/shard_map/ppermute | solution.py:22
  116.6 3.9 %collective-permute-start.2 = (bf16[16,1792]{1,0:T(8,128)(2,1)S(1)}, bf16[16,1792]{1,0:T(8,128)(2,1)S(1)}, u32[]{:S(2)}, u32[]{:S(2)}) collective-permute-start(bf16[16,1792]{1,0:T(8,128)(2,1)S(1)} %collective-permute-done.1), channel_id=1, source_target_pairs={{0,16},{16,32},{32,48},{48,64},{64,80},{80,96},{96,112},{112,128},... | collective-permute-start | bytes 172040 | tf_op jit(solution)/shard_map/ppermute | solution.py:20
  119.2 3.6 %collective-permute-start.9 = (bf16[16,1792]{1,0:T(8,128)(2,1)S(1)}, bf16[16,1792]{1,0:T(8,128)(2,1)S(1)}, u32[]{:S(2)}, u32[]{:S(2)}) collective-permute-start(bf16[16,1792]{1,0:T(8,128)(2,1)S(1)} %collective-permute-done.8), channel_id=1, source_target_pairs={{0,240},{16,0},{32,16},{48,32},{64,48},{80,64},{96,80},{112,96},{1... | collective-permute-start | bytes 172040 | tf_op jit(solution)/shard_map/ppermute | solution.py:22
  120.5 4.8 %collective-permute-start.3 = (bf16[16,1792]{1,0:T(8,128)(2,1)S(1)}, bf16[16,1792]{1,0:T(8,128)(2,1)S(1)}, u32[]{:S(2)}, u32[]{:S(2)}) collective-permute-start(bf16[16,1792]{1,0:T(8,128)(2,1)S(1)} %collective-permute-done.2), channel_id=1, source_target_pairs={{0,16},{16,32},{32,48},{48,64},{64,80},{80,96},{96,112},{112,128},... | collective-permute-start | bytes 172040 | tf_op jit(solution)/shard_map/ppermute | solution.py:20
  122.8 4.0 %collective-permute-start.10 = (bf16[16,1792]{1,0:T(8,128)(2,1)S(1)}, bf16[16,1792]{1,0:T(8,128)(2,1)S(1)}, u32[]{:S(2)}, u32[]{:S(2)}) collective-permute-start(bf16[16,1792]{1,0:T(8,128)(2,1)S(1)} %collective-permute-done.9), channel_id=1, source_target_pairs={{0,240},{16,0},{32,16},{48,32},{64,48},{80,64},{96,80},{112,96},{1... | collective-permute-start | bytes 172040 | tf_op jit(solution)/shard_map/ppermute | solution.py:22
  125.3 4.8 %collective-permute-start.4 = (bf16[16,1792]{1,0:T(8,128)(2,1)S(1)}, bf16[16,1792]{1,0:T(8,128)(2,1)S(1)}, u32[]{:S(2)}, u32[]{:S(2)}) collective-permute-start(bf16[16,1792]{1,0:T(8,128)(2,1)S(1)} %collective-permute-done.3), channel_id=1, source_target_pairs={{0,16},{16,32},{32,48},{48,64},{64,80},{80,96},{96,112},{112,128},... | collective-permute-start | bytes 172040 | tf_op jit(solution)/shard_map/ppermute | solution.py:20
  126.8 4.0 %collective-permute-start.11 = (bf16[16,1792]{1,0:T(8,128)(2,1)S(1)}, bf16[16,1792]{1,0:T(8,128)(2,1)S(1)}, u32[]{:S(2)}, u32[]{:S(2)}) collective-permute-start(bf16[16,1792]{1,0:T(8,128)(2,1)S(1)} %collective-permute-done.10), channel_id=1, source_target_pairs={{0,240},{16,0},{32,16},{48,32},{64,48},{80,64},{96,80},{112,96},{1... | collective-permute-start | bytes 172040 | tf_op jit(solution)/shard_map/ppermute | solution.py:22
  130.1 4.8 %collective-permute-start.5 = (bf16[16,1792]{1,0:T(8,128)(2,1)S(1)}, bf16[16,1792]{1,0:T(8,128)(2,1)S(1)}, u32[]{:S(2)}, u32[]{:S(2)}) collective-permute-start(bf16[16,1792]{1,0:T(8,128)(2,1)S(1)} %collective-permute-done.4), channel_id=1, source_target_pairs={{0,16},{16,32},{32,48},{48,64},{64,80},{80,96},{96,112},{112,128},... | collective-permute-start | bytes 172040 | tf_op jit(solution)/shard_map/ppermute | solution.py:20
  130.8 4.7 %collective-permute-start.12 = (bf16[16,1792]{1,0:T(8,128)(2,1)S(1)}, bf16[16,1792]{1,0:T(8,128)(2,1)S(1)}, u32[]{:S(2)}, u32[]{:S(2)}) collective-permute-start(bf16[16,1792]{1,0:T(8,128)(2,1)S(1)} %collective-permute-done.11), channel_id=1, source_target_pairs={{0,240},{16,0},{32,16},{48,32},{64,48},{80,64},{96,80},{112,96},{1... | collective-permute-start | bytes 172040 | tf_op jit(solution)/shard_map/ppermute | solution.py:22
  135.0 4.9 %collective-permute-start.6 = (bf16[16,1792]{1,0:T(8,128)(2,1)S(1)}, bf16[16,1792]{1,0:T(8,128)(2,1)S(1)}, u32[]{:S(2)}, u32[]{:S(2)}) collective-permute-start(bf16[16,1792]{1,0:T(8,128)(2,1)S(1)} %collective-permute-done.5), channel_id=1, source_target_pairs={{0,16},{16,32},{32,48},{48,64},{64,80},{80,96},{96,112},{112,128},... | collective-permute-start | bytes 172040 | tf_op jit(solution)/shard_map/ppermute | solution.py:20
  135.5 5.2 %collective-permute-start.13 = (bf16[16,1792]{1,0:T(8,128)(2,1)S(1)}, bf16[16,1792]{1,0:T(8,128)(2,1)S(1)}, u32[]{:S(2)}, u32[]{:S(2)}) collective-permute-start(bf16[16,1792]{1,0:T(8,128)(2,1)S(1)} %collective-permute-done.12), channel_id=1, source_target_pairs={{0,240},{16,0},{32,16},{48,32},{64,48},{80,64},{96,80},{112,96},{1... | collective-permute-start | bytes 172040 | tf_op jit(solution)/shard_map/ppermute | solution.py:22
  139.8 5.2 %collective-permute-start.7 = (bf16[16,1792]{1,0:T(8,128)(2,1)S(1)}, bf16[16,1792]{1,0:T(8,128)(2,1)S(1)}, u32[]{:S(2)}, u32[]{:S(2)}) collective-permute-start(bf16[16,1792]{1,0:T(8,128)(2,1)S(1)} %collective-permute-done.6), channel_id=1, source_target_pairs={{0,16},{16,32},{32,48},{48,64},{64,80},{80,96},{96,112},{112,128},... | collective-permute-start | bytes 172040 | tf_op jit(solution)/shard_map/ppermute | solution.py:20
  140.7 13.7 %collective-permute-start.14 = (bf16[16,1792]{1,0:T(8,128)(2,1)S(1)}, bf16[16,1792]{1,0:T(8,128)(2,1)S(1)}, u32[]{:S(2)}, u32[]{:S(2)}) collective-permute-start(bf16[16,1792]{1,0:T(8,128)(2,1)S(1)} %collective-permute-done.13), channel_id=1, source_target_pairs={{0,240},{16,0},{32,16},{48,32},{64,48},{80,64},{96,80},{112,96},{1... | collective-permute-start | bytes 172040 | tf_op jit(solution)/shard_map/ppermute | solution.py:22
Sparse Core Ops, SparseCore 0:
  88.8 53.4 all-gather.2
